TPU v7x, 256 devices: a whole 4x4x8 slice. The times are simulated.
256 devices in a mesh: gx: 16 (over z, core), gy: 16 (over x, y).
Axes of the slice: x: 4, y: 4, z: 8, core: 2. Of those that a mesh axis runs over, the one named last changes fastest.
Arguments:
- positions: float32 [16, 16, 3, 256], P('gx', 'gy'), may hold values from 0 to 10
- species: int32 [16, 16, 256], P('gx', 'gy'), may hold values from 0 to 5
- neighbours: int32 [16, 16, 256, 12], P('gx', 'gy'), may hold values from 0 to 2303
- counts: int32 [16, 16, 256], P('gx', 'gy'), may hold values from 6 to 12
- species_embed: float32 [6, 128], replicated, may hold values from -6 to 6
- radial: float32 [2, 2, 8, 128], replicated, may hold values from -2 to 2
- mixing: float32 [2, 2, 128, 128], replicated, may hold values from -0.5 to 0.5
- read_hidden: float32 [128, 128], replicated, may hold values from -0.5 to 0.5
- read_out: float32 [128], replicated, may hold values from -0.5 to 0.5
- charge_map: float32 [128, 64], replicated, may hold values from -0.5 to 0.5
- wavevectors: int32 [3, 4096], replicated, may hold values from -8 to 8, as said below
Outputs:
- forces: float32 [16, 16, 3, 256], P('gx', 'gy')
- site_energy: float32 [16, 16, 256], P('gx', 'gy')
Inputs may be any that keep to these rules, and one draw needn't show every extreme that they name: `neighbours`: entry (3 a + b) * 256 + t names atom t of the cell offset by (a - 1, b - 1) along gx, gy, periodically. Slots n < counts are used. `wavevectors`: the 4096 triples are distinct, and no triple has its first two components both zero.
All inputs are finite; a program needn't handle non-finite values.
Results may differ from a plain program's by a relative error of at most 0.0017.
Values may be sent and summed in bfloat16 or wider, within the bound.
A program may use at most 128 MiB of HBM per device.

v0:
```python
import math
import jax
import jax.numpy as jnp
from jax import lax
from jax.sharding import PartitionSpec as P

cell_width = 10.0
box_height = 30.0
cut_radius = 50.0
soften = 0.25
screen = 0.5
smear_width = 0.5
highest = lax.Precision.HIGHEST


def passed_along(block, axis, distance):
    devices = range(lax.axis_size(axis))
    route = [((i - distance) % len(devices), i) for i in devices]
    return lax.ppermute(block, axis, route)


def with_halo(block, sides, width):
    for axis, dim in sides:
        count = lax.axis_size(axis)
        forward = [(i, i + 1) for i in range(count - 1)]
        forward.append((count - 1, 0))
        backward = [(target, source) for source, target in forward]
        low = lax.ppermute(
            lax.slice_in_dim(block, block.shape[dim] - width, None, axis=dim), axis, forward
        )
        high = lax.ppermute(lax.slice_in_dim(block, 0, width, axis=dim), axis, backward)
        block = jnp.concatenate([low, block, high], axis=dim)
    return block


def build_frame(extended):
    offsets = (jnp.arange(3, dtype=jnp.float32) - 1.0) * cell_width
    shift_x = jnp.broadcast_to(offsets[:, None], (3, 3))
    shift_y = jnp.broadcast_to(offsets[None, :], (3, 3))
    shifts = jnp.stack([shift_x, shift_y, jnp.zeros((3, 3), jnp.float32)], axis=2)
    coords = extended[:, :, :3, :] + shifts[:, :, :, None]
    src_pos = jnp.moveaxis(coords, 2, 0).reshape(3, -1)
    kind_codes = extended[:, :, 3, :].reshape(-1)
    return (src_pos, kind_codes)


def embed_rows(kind_codes, species_embed):
    lookup = (
        kind_codes[:, None] == jnp.arange(species_embed.shape[0], dtype=jnp.float32)[None, :]
    ).astype(jnp.float32)
    return jnp.dot(lookup, species_embed, precision=highest)


def interact(h_dst, h_src, own_pos, src_pos, neighbour_ids, slot_counts, radial_pair, mix_pair):
    slots = neighbour_ids.shape[1]
    orders = radial_pair.shape[1]
    relative = src_pos[:, neighbour_ids] - own_pos[:, :, None]
    distance = jnp.sqrt(jnp.sum(relative * relative, axis=0) + soften)
    unit_vec = relative / distance[None]
    frequency = jnp.arange(1, orders + 1, dtype=jnp.float32) * (math.pi / cut_radius)
    arg_scaled = distance[:, :, None] * frequency
    radial_basis = jnp.sin(arg_scaled) / arg_scaled
    live_slots = (jnp.arange(slots)[None, :] < slot_counts[:, None]).astype(jnp.float32)
    weight_zero = (
        jnp.einsum("anr,rc->anc", radial_basis, radial_pair[0], precision=highest)
        * live_slots[:, :, None]
    )
    weight_one = (
        jnp.einsum("anr,rc->anc", radial_basis, radial_pair[1], precision=highest)
        * live_slots[:, :, None]
    )
    source = h_src[neighbour_ids]
    norm_factor = 1.0 / math.sqrt(slots)
    msg_zero = jnp.sum(weight_zero * source, axis=1) * norm_factor
    msg_one = (
        jnp.einsum("anc,xan->xac", weight_one * source, unit_vec, precision=highest) * norm_factor
    )
    squares = jnp.sum(msg_one * msg_one, axis=0)
    preact = jnp.dot(msg_zero, mix_pair[0], precision=highest) + jnp.dot(
        squares, mix_pair[1], precision=highest
    )
    return h_dst + jax.nn.silu(preact)


def first_layer(own_pos, src_pos, initial_src, neighbour_ids, slot_counts, radial, mixing):
    atom_count = own_pos.shape[1]
    return interact(
        initial_src[4 * atom_count : 5 * atom_count],
        initial_src,
        own_pos,
        src_pos,
        neighbour_ids,
        slot_counts,
        radial[0],
        mixing[0],
    )


def second_section(
    hidden_src,
    own_pos,
    src_pos,
    neighbour_ids,
    slot_counts,
    radial,
    mixing,
    read_hidden,
    read_out,
    charge_map,
):
    atom_count = own_pos.shape[1]
    hidden_two = interact(
        hidden_src[4 * atom_count : 5 * atom_count],
        hidden_src,
        own_pos,
        src_pos,
        neighbour_ids,
        slot_counts,
        radial[1],
        mixing[1],
    )
    energy = jnp.dot(
        jax.nn.silu(jnp.dot(hidden_two, read_hidden, precision=highest)),
        read_out,
        precision=highest,
    )
    charges = jnp.dot(hidden_two, charge_map, precision=highest)
    return (energy, charges)


def wave_terms(wavevectors, grid_x, grid_y):
    lengths = jnp.array([grid_x * cell_width, grid_y * cell_width, box_height], dtype=jnp.float32)
    wave_phys = 2.0 * math.pi * wavevectors.astype(jnp.float32) / lengths[:, None]
    wave_sq = jnp.sum(wave_phys * wave_phys, axis=0)
    green_weight = jnp.exp(-smear_width * wave_sq) / (wave_sq + screen * screen)
    return (wave_phys, green_weight)


def phase_pair(global_pos, wave_part):
    angle = (
        global_pos[0][:, None] * wave_part[0][None, :]
        + global_pos[1][:, None] * wave_part[1][None, :]
        + global_pos[2][:, None] * wave_part[2][None, :]
    )
    return (jnp.cos(angle), jnp.sin(angle))


def structure_term(charges, global_pos, wave_part):
    cosine, sine_part = phase_pair(global_pos, wave_part)
    dims = (((0,), (0,)), ((), ()))
    real_part = lax.dot_general(cosine, charges, dims, precision=highest)
    imag_part = lax.dot_general(sine_part, charges, dims, precision=highest)
    return jnp.concatenate([real_part, imag_part], axis=1)


def fold_terms(carried, piece_rows, start_row, charges, global_pos, wave_phys):
    potential, lr_grad = carried
    row_count = piece_rows.shape[0]
    lat_width = charges.shape[1]
    wave_part = lax.dynamic_slice_in_dim(
        wave_phys, jnp.asarray(start_row).astype(jnp.int32), row_count, 1
    )
    cosine, sine_part = phase_pair(global_pos, wave_part)
    weight_re = piece_rows[:, :lat_width]
    weight_im = piece_rows[:, lat_width:]
    potential = (
        potential
        + jnp.dot(cosine, weight_re, precision=highest)
        + jnp.dot(sine_part, weight_im, precision=highest)
    )
    dims = (((1,), (1,)), ((), ()))
    proj_re = lax.dot_general(charges, weight_re, dims, precision=highest)
    proj_im = lax.dot_general(charges, weight_im, dims, precision=highest)
    phase_turn = cosine * proj_im - sine_part * proj_re
    lr_grad = lr_grad + lax.dot_general(wave_part, phase_turn, dims, precision=highest)
    return (potential, lr_grad)


def send_back(cotangent_grid):
    column = cotangent_grid[:, 1]
    for shift_by, column_pick in ((1, 2), (-1, 0)):
        column = column + passed_along(cotangent_grid[:, column_pick], "gy", shift_by)
    running = column[1]
    for shift_by, column_pick in ((1, 2), (-1, 0)):
        running = running + passed_along(column[column_pick], "gx", shift_by)
    return running


def per_device(
    positions,
    species,
    neighbours,
    counts,
    species_embed,
    radial,
    mixing,
    read_hidden,
    read_out,
    charge_map,
    wavevectors,
):
    atom_count = positions.shape[3]
    width = read_hidden.shape[0]
    lat_width = charge_map.shape[1]
    wave_count = wavevectors.shape[1]
    own_pos = positions[0, 0]
    neighbour_ids = neighbours[0, 0]
    slot_counts = counts[0, 0]
    packed = jnp.concatenate([positions, species.astype(jnp.float32)[:, :, None, :]], axis=2)
    extended = with_halo(packed, (("gx", 0), ("gy", 1)), 1)
    src_pos, kind_codes = build_frame(extended)
    initial_src = embed_rows(kind_codes, species_embed)

    def layer_one(own_coords, source_coords):
        return first_layer(
            own_coords, source_coords, initial_src, neighbour_ids, slot_counts, radial, mixing
        )

    hidden_one, pull_one = jax.vjp(layer_one, own_pos, src_pos)
    hidden_low = hidden_one.astype(jnp.bfloat16)
    ghost_hidden = with_halo(hidden_low[None, None], (("gx", 0), ("gy", 1)), 1)
    hidden_src = ghost_hidden.reshape(9 * atom_count, width).astype(jnp.float32)

    def section_two(source_hidden, own_coords, source_coords):
        return second_section(
            source_hidden,
            own_coords,
            source_coords,
            neighbour_ids,
            slot_counts,
            radial,
            mixing,
            read_hidden,
            read_out,
            charge_map,
        )

    (energy_sr, charges), pull_two = jax.vjp(section_two, hidden_src, own_pos, src_pos)
    grid_x = lax.axis_size("gx")
    grid_y = lax.axis_size("gy")
    row_index = lax.axis_index("gx")
    col_index = lax.axis_index("gy")
    anchor = jnp.stack(
        [
            row_index.astype(jnp.float32) * cell_width,
            col_index.astype(jnp.float32) * cell_width,
            jnp.zeros((), jnp.float32),
        ]
    )
    global_pos = own_pos + anchor[:, None]
    wave_phys, green_weight = wave_terms(wavevectors, grid_x, grid_y)
    start_state = (
        jnp.zeros((atom_count, lat_width), jnp.float32),
        jnp.zeros((3, atom_count), jnp.float32),
    )

    def fold_piece(carried, piece_rows, start_row):
        return fold_terms(carried, piece_rows, start_row, charges, global_pos, wave_phys)

    block_rows = math.gcd(wave_count, 512)
    block_total = wave_count // block_rows

    def term_block(block_idx):
        return structure_term(
            charges,
            global_pos,
            lax.dynamic_slice_in_dim(wave_phys, block_idx * block_rows, block_rows, 1),
        )

    partial_sf = lax.map(term_block, jnp.arange(block_total)).reshape(wave_count, 2 * lat_width)
    structure = lax.psum(partial_sf, ("gx", "gy"))
    weighted = green_weight[:, None] * structure

    def fold_block(block_idx, carried):
        start_row = block_idx * block_rows
        return fold_piece(
            carried, lax.dynamic_slice_in_dim(weighted, start_row, block_rows, 0), start_row
        )

    potential, lr_grad = lax.fori_loop(0, block_total, fold_block, start_state)
    lr_scale = 1.0 / math.sqrt(wave_count * lat_width * atom_count * grid_x * grid_y)
    site_energy = energy_sr + lr_scale * jnp.sum(charges * potential, axis=1)
    grad_hidden, grad_own_two, grad_src_two = pull_two(
        (jnp.ones_like(energy_sr), 2.0 * lr_scale * potential)
    )
    grad_hidden_own = send_back(grad_hidden.reshape(3, 3, atom_count, width))
    grad_own_one, grad_src_one = pull_one(grad_hidden_own)
    grad_src = jnp.moveaxis((grad_src_one + grad_src_two).reshape(3, 3, 3, atom_count), 0, 2)
    grad_back = send_back(grad_src)
    forces = -(grad_own_one + grad_own_two + grad_back + 2.0 * lr_scale * lr_grad)
    return (forces[None, None], site_energy[None, None])


def solution(mesh):
    in_specs = (
        P("gx", "gy", None, None),
        P("gx", "gy", None),
        P("gx", "gy", None, None),
        P("gx", "gy", None),
        P(),
        P(),
        P(),
        P(),
        P(),
        P(),
        P(),
    )
    out_specs = (P("gx", "gy", None, None), P("gx", "gy", None))
    return jax.shard_map(
        per_device, mesh=mesh, in_specs=in_specs, out_specs=out_specs, check_vma=False
    )
```

profile of v0, /device:TPU:127, one launch (start us, length us, event | category | flops | bytes accessed | tf_op | source)
XLA Modules:
  0.0 658.0 jit_solution(15282596504475978514)
XLA Ops:
  9.3 2.7 collective-permute-start
  17.3 4.3 collective-permute-start.2
  24.4 8.1 %gather_fusion = f32[3072,3]{1,0:T(8,128)S(1)} fusion(f32[3,2304]{0,1:T(8,128)S(1)} %bitcast.271, s32[3072]{0:T(1024)S(1)} %broadcast_clamp_fusion), kind=kCustom, calls=%fused_computation | custom fusion | bytes 86016 | tf_op jit(solution)/shard_map/jvp()/gather | solution.py:57
  36.6 10.8 %gather_fusion.1 = f32[3072,128]{1,0:T(8,128)} fusion(f32[2304,128]{1,0:T(8,128)S(1)} %fusion.133, s32[3072]{0:T(1024)S(1)} %broadcast_clamp_fusion), kind=kCustom, calls=%fused_computation.1 | custom fusion | bytes 3158016 | tf_op jit(solution)/shard_map/jvp()/gather | solution.py:72
  49.1 4.2 multiply_reduce_fusion.1
  53.3 4.4 multiply_multiply_fusion
  58.0 4.0 multiply_reduce_fusion.3
  62.3 2.9 collective-permute-start.4
  67.3 5.2 collective-permute-start.6
  72.5 5.0 convolution_multiply_fusion.1
  77.7 10.8 %gather_fusion.2 = f32[3072,128]{1,0:T(8,128)} fusion(f32[2304,128]{1,0:T(8,128)S(1)} %bitcast_convert_fusion, s32[3072]{0:T(1024)S(1)} %broadcast_clamp_fusion), kind=kCustom, calls=%fused_computation.2 | custom fusion | bytes 3158016 | tf_op jit(solution)/shard_map/jvp()/gather | solution.py:72
  90.0 6.9 %copy_multiply_fusion.1 = (f32[256,12,128]{2,0,1:T(8,128)S(1)}, f32[256,128]{1,0:T(8,128)S(1)}, f32[256,12,128]{2,0,1:T(8,128)}) fusion(f32[256,12,128]{2,1,0:T(8,128)S(1)} %reshape.168, f32[256,12,128]{2,0,1:T(8,128)} %convolution_multiply_fusion.1, f32[256,12]{0,1:T(8,128)S(1)} %fusion.161, f32[2,2,8,128]{3,2,1,0:T(8,128)} %param.21, ...), kind=kOutput, calls=%fused_computation.121 | convolution fusion | flops 39337984 | bytes 6451232 | tf_op jit(solution)/shard_map/jvp(anr,rc->anc)/dot_general | solution.py:69
  97.2 3.9 multiply_reduce_fusion.2
  102.4 62.1 %while.26 = (s32[]{:T(128)}, f32[8,512,128]{2,1,0:T(8,128)}, f32[3,256]{1,0:T(4,128)S(1)}, s32[8]{0:T(128)S(1)}, f32[3,4096]{1,0:T(4,128)}, /*index=5*/f32[256,6...) while((s32[]{:T(128)}, f32[8,512,128]{2,1,0:T(8,128)}, ...), condition=%wide.region_7.8_spmd, body=%wide.region_6.7_spmd.sunk | while | flops 202702848 | bytes 2003167 | solution.py:270
  166.3 260.0 %all-reduce.3.cloned.1.call-done = f32[4096,128]{1,0:T(8,128)} async-done(((f32[4096,128]{1,0:T(8,128)}), f32[4096,128]{1,0:T(8,128)}) %all-reduce.3.cloned.1.call-update) | async-done | bytes 2097168 | tf_op jit(solution)/shard_map/psum | solution.py:271
  428.5 87.4 %while.27 = (s32[]{:T(128)}, f32[256,64]{0,1:T(8,128)S(1)}, f32[3,256]{1,0:T(4,128)S(1)}, f32[3,256]{1,0:T(4,128)S(1)}, f32[3,4096]{1,0:T(4,128)}, /*index=5*/f3...) while((s32[]{:T(128)}, f32[256,64]{0,1:T(8,128)S(1)}, ...), condition=%wide.region_10.11_spmd.clone, body=%wide.region_9.10_spmd.clone.sunk | while | flops 410437120 | bytes 3739922 | solution.py:280
  518.0 4.0 fusion.88
  527.2 17.4 %scatter_fusion = f32[2304,128]{1,0:T(8,128)S(1)} fusion(f32[2304,128]{1,0:T(8,128)S(1)} %pad.3, s32[3072]{0:T(1024)S(1)} %reshape.153, f32[3072,128]{1,0:T(8,128)S(1)} %reshape.179), kind=kCustom, calls=%fused_computation.3 | custom fusion | flops 393216 | bytes 4730880 | tf_op jit(solution)/shard_map/transpose(jvp())/scatter-add | solution.py:72
  550.7 4.7 collective-permute-done.8
  555.4 3.8 collective-permute-done.9
  561.1 3.7 fusion.125
  568.0 4.1 fusion.47
  572.1 5.3 fusion.89
  577.4 6.2 fusion.80
  586.8 3.9 fusion.52
  590.8 3.1 fusion.122
  594.2 3.0 fusion.201
  598.4 17.2 %scatter_custom_fusion.1 = f32[3,2304]{0,1:T(8,128)S(1)} fusion(s32[3072]{0:T(1024)S(1)} %reshape.153, f32[3072,3]{1,0:T(8,128)S(1)} %copy.264, f32[]{:T(128)} %constant.47.clone.1), kind=kCustom, calls=%fused_computation.107 | custom fusion | flops 9216 | bytes 27652 | tf_op jit(solution)/shard_map/transpose(jvp())/scatter-add | solution.py:57
  617.3 17.5 %scatter_custom_fusion.2 = f32[3,2304]{0,1:T(8,128)S(1)} fusion(s32[3072]{0:T(1024)S(1)} %reshape.153, f32[3072,3]{1,0:T(8,128)} %copy.266, f32[]{:T(128)} %constant.47.clone.1), kind=kCustom, calls=%fused_computation.105 | custom fusion | flops 9216 | bytes 28160 | tf_op jit(solution)/shard_map/transpose(jvp())/scatter-add | solution.py:57
  640.6 3.1 collective-permute-done.13
  643.7 2.4 collective-permute-start.14
  646.8 3.5 collective-permute-done.15
  (340 shorter events, 200.1 us)
Async XLA Ops:
  7.2 158.8 %copy-start = (f32[128,128]{1,0:T(8,128)S(1)}, f32[128,128]{1,0:T(8,128)}, u32[]{:S(2)}) copy-start(f32[128,128]{1,0:T(8,128)} %param.23) | copy-start | bytes 196612
  7.2 419.1 %all-reduce.3.cloned.1.call-start = ((), (), s32[]{:S(2)}) async-start(), calls=%async_computation | async-start | bytes 4194304 | tf_op jit(solution)/shard_map/psum | solution.py:271
  8.6 7.5 %collective-permute-start.1 = (f32[1,1,4,256]{3,1,2,0:T(1,128)S(1)}, f32[1,1,4,256]{3,1,2,0:T(1,128)S(1)}, u32[]{:S(2)}, u32[]{:S(2)}) collective-permute-start(f32[1,1,4,256]{3,1,2,0:T(1,128)S(1)} %pad_maximum_fusion.5), channel_id=1, source_target_pairs={{16,0},{32,16},{48,32},{64,48},{80,64},{96,80},{112,96},{128,112},... | collective-permute-start | bytes 12296 | tf_op jit(solution)/shard_map/ppermute | solution.py:31
  9.3 6.8 %collective-permute-start = (f32[1,1,4,256]{3,1,2,0:T(1,128)S(1)}, f32[1,1,4,256]{3,1,2,0:T(1,128)S(1)}, u32[]{:S(2)}, u32[]{:S(2)}) collective-permute-start(f32[1,1,4,256]{3,1,2,0:T(1,128)S(1)} %pad_maximum_fusion.5), channel_id=1, source_target_pairs={{0,16},{16,32},{32,48},{48,64},{64,80},{80,96},{96,112},{112,128},... | collective-permute-start | bytes 12296 | tf_op jit(solution)/shard_map/ppermute | solution.py:28
  16.8 6.3 collective-permute-start.3
  17.3 5.8 collective-permute-start.2
  49.1 8.6 %copy-start.4 = (f32[256,12,128]{2,1,0:T(8,128)}, f32[256,12,128]{2,1,0:T(8,128)S(1)}, u32[]{:S(2)}) copy-start(f32[256,12,128]{2,1,0:T(8,128)S(1)} %reshape.160) | copy-start | bytes 4718596
  58.0 7.3 %copy-start.39 = (f32[1,1,3,256]{3,1,2,0:T(1,128)S(1)}, f32[1,1,3,256]{3,1,2,0:T(1,128)}, u32[]{:S(2)}) copy-start(f32[1,1,3,256]{3,1,2,0:T(1,128)} %param.16) | copy-start | bytes 9220
  58.0 7.3 %copy-start.48 = (f32[3]{0:T(128)S(1)}, f32[3]{0:T(128)}, u32[]{:S(2)}) copy-start(f32[3]{0:T(128)} %pad_maximum_fusion.6) | copy-start | bytes 40
  62.2 15.3 %copy-start.17 = (f32[256,128]{1,0:T(8,128)}, f32[256,128]{1,0:T(8,128)S(1)}, u32[]{:S(2)}) copy-start(f32[256,128]{1,0:T(8,128)S(1)} %convolution_add_fusion.5) | copy-start | bytes 393220
  62.3 4.9 collective-permute-start.5
  62.3 4.9 collective-permute-start.4
  67.2 10.2 %collective-permute-start.7 = (bf16[3,1,256,128]{3,2,1,0:T(8,128)(2,1)S(1)}, bf16[3,1,256,128]{3,2,1,0:T(8,128)(2,1)S(1)}, u32[]{:S(2)}, u32[]{:S(2)}) collective-permute-start(bf16[3,1,256,128]{3,2,1,0:T(8,128)(2,1)S(1)} %pad_maximum_fusion.1), channel_id=1, source_target_pairs={{1,0},{2,1},{3,2},{4,3},{5,4},{6,5},{7,6},{8,7},{9,8},{10,9},{11,1... | collective-permute-start | bytes 589832 | tf_op jit(solution)/shard_map/ppermute | solution.py:31
  67.3 10.1 %collective-permute-start.6 = (bf16[3,1,256,128]{3,2,1,0:T(8,128)(2,1)S(1)}, bf16[3,1,256,128]{3,2,1,0:T(8,128)(2,1)S(1)}, u32[]{:S(2)}, u32[]{:S(2)}) collective-permute-start(bf16[3,1,256,128]{3,2,1,0:T(8,128)(2,1)S(1)} %pad_maximum_fusion.1), channel_id=1, source_target_pairs={{0,1},{1,2},{2,3},{3,4},{4,5},{5,6},{6,7},{7,8},{8,9},{9,10},{10,1... | collective-permute-start | bytes 589832 | tf_op jit(solution)/shard_map/ppermute | solution.py:28
  90.0 7.2 %copy-start.12 = (f32[256,12,3]{1,0,2:T(8,128)S(1)}, f32[256,12,3]{1,0,2:T(8,128)}, u32[]{:S(2)}) copy-start(f32[256,12,3]{1,0,2:T(8,128)} %copy-done.10) | copy-start | bytes 110596
  90.0 7.2 %copy-start.27 = (f32[256,12]{1,0:T(8,128)S(1)}, f32[256,12]{1,0:T(8,128)}, u32[]{:S(2)}) copy-start(f32[256,12]{1,0:T(8,128)} %copy.232) | copy-start | bytes 36868
  166.3 350.0 %copy-start.52 = (f32[256,128]{1,0:T(8,128)}, f32[256,128]{1,0:T(8,128)S(1)}, u32[]{:S(2)}) copy-start(f32[256,128]{1,0:T(8,128)S(1)} %fusion.196) | copy-start | bytes 393220
  428.5 88.0 %copy-start.50 = (f32[128]{0:T(128)S(1)}, f32[128]{0:T(128)}, u32[]{:S(2)}) copy-start(f32[128]{0:T(128)} %param.24) | copy-start | bytes 1540
  428.5 88.3 %copy-start.21 = (f32[2,2,128,128]{3,2,1,0:T(8,128)S(1)}, f32[2,2,128,128]{3,2,1,0:T(8,128)}, u32[]{:S(2)}) copy-start(f32[2,2,128,128]{3,2,1,0:T(8,128)} %param.22) | copy-start | bytes 786436
  527.2 19.5 %copy-start.51 = (f32[128]{0:T(128)S(1)}, f32[128]{0:T(128)}, u32[]{:S(2)}) copy-start(f32[128]{0:T(128)} %param.24) | copy-start | bytes 1540
  544.6 10.7 %collective-permute-start.8 = (f32[3,256,128]{2,1,0:T(8,128)S(1)}, f32[3,256,128]{2,1,0:T(8,128)S(1)}, u32[]{:S(2)}, u32[]{:S(2)}) collective-permute-start(f32[3,256,128]{2,1,0:T(8,128)S(1)} %get-tuple-element.335), channel_id=1, source_target_pairs={{15,0},{0,1},{1,2},{2,3},{3,4},{4,5},{5,6},{6,7},{7,8},{8,9},{9,10... | collective-permute-start | bytes 1179656 | tf_op jit(solution)/shard_map/ppermute | solution.py:19
  546.7 12.5 %collective-permute-start.9 = (f32[3,256,128]{2,1,0:T(8,128)S(1)}, f32[3,256,128]{2,1,0:T(8,128)S(1)}, u32[]{:S(2)}, u32[]{:S(2)}) collective-permute-start(f32[3,256,128]{2,1,0:T(8,128)S(1)} %get-tuple-element.336), channel_id=1, source_target_pairs={{1,0},{2,1},{3,2},{4,3},{5,4},{6,5},{7,6},{8,7},{9,8},{10,9},{11,1... | collective-permute-start | bytes 1179656 | tf_op jit(solution)/shard_map/ppermute | solution.py:19
  548.4 12.6 %copy-start.15 = (f32[256,12,128]{2,1,0:T(8,128)S(1)}, f32[256,12,128]{2,1,0:T(8,128)}, u32[]{:S(2)}) copy-start(f32[256,12,128]{2,1,0:T(8,128)} %copy-done.14) | copy-start | bytes 4718596
  559.3 5.4 collective-permute-start.10
  561.0 5.6 collective-permute-start.11
  577.4 9.4 %copy-start.5 = (f32[256,12,128]{2,1,0:T(8,128)S(1)}, f32[256,12,128]{2,1,0:T(8,128)}, u32[]{:S(2)}) copy-start(f32[256,12,128]{2,1,0:T(8,128)} %copy-done.4) | copy-start | bytes 4718596
  634.8 11.3 %copy-start.49 = (f32[1,256]{1,0:T(1,128)S(1)}, f32[1,256]{1,0:T(1,128)}, u32[]{:S(2)}) copy-start(f32[1,256]{1,0:T(1,128)} %fusion.112) | copy-start | bytes 3076
  634.8 11.8 %copy-start.31 = (f32[3,256]{0,1:T(8,128)S(1)}, f32[3,256]{0,1:T(8,128)}, u32[]{:S(2)}) copy-start(f32[3,256]{0,1:T(8,128)} %get-tuple-element.317) | copy-start | bytes 9220
  637.7 2.9 collective-permute-start.12
  637.8 5.9 collective-permute-start.13
  643.7 3.1 collective-permute-start.14
  646.1 4.2 collective-permute-start.15
  (38 other events, 145.1 us)
Sparse Core Ops, SparseCore 0:
  164.6 261.6 all-reduce.2
where the time goes:
time: 664 us; the launch traced here: 658 us
  waiting for transfers between devices  280 us (42%)
  matrix products  184 us (28%)
  local copies, waits for them, and re-layouts  78.6 us (12%)
  other arithmetic  68.8 us (10%)
  starting transfers between devices  24.2 us (4%)
  between operations  15.2 us (2%)
    psum x1, waiting for transfers between devices, per_device(): structure = lax.psum(partial_sf, ('gx', 'gy'))  260 us
    scatter-add x2, other arithmetic, interact(): relative = src_pos[:, neighbour_ids] - own_pos[:, :, None]  34.7 us
    dot_general x6, matrix products, interact(): jnp.einsum('anc,xan->xac', weight_one * source, unit_vec, precision=highest)  27.5 us
    gather x4, local copies, waits for them, and re-layouts, interact(): source = h_src[neighbour_ids]  24.7 us
    dot_general x4, matrix products, interact(): jnp.einsum('anr,rc->anc', radial_basis, radial_pair[1], precision=highest)  18.9 us
    dot_general x8, matrix products, structure_term(): imag_part = lax.dot_general(sine_part, charges, dims, precision=highest)  18.9 us
    dot_general x8, matrix products, fold_terms(): jnp.dot(sine_part, weight_im, precision=highest)  18.7 us
    dot_general x8, matrix products, structure_term(): real_part = lax.dot_general(cosine, charges, dims, precision=highest)  18.7 us
  transfers between devices with their start and end apart: 17, of which 8 were waited for; matrix products, arithmetic and copies ran while one was open for 3% of the time, Pallas kernels for 0%

commit v1 on v0

--- a/solution.py
+++ b/solution.py
@@ -268,7 +268,8 @@
         )
 
     partial_sf = lax.map(term_block, jnp.arange(block_total)).reshape(wave_count, 2 * lat_width)
-    structure = lax.psum(partial_sf, ("gx", "gy"))
+    blocks_find = lambda block_here: lax.psum(lax.psum(block_here, axis_name="gy"), axis_name="gx")
+    structure = blocks_find(partial_sf)
     weighted = green_weight[:, None] * structure
 
     def fold_block(block_idx, carried):

time: 664 us -> 620 us (0.934)
  waiting for transfers between devices: 280 us -> 238 us
    psum x1 -> x2, waiting for transfers between devices: 260 us -> 217 us  [the longest x1 119 us: per_device(): lax.psum(lax.psum(block_here, axis_name='gy'), axis_name='gx')]
  transfers between devices with their start and end apart: 17 -> 18, of which waited for: 8 -> 9; matrix products, arithmetic and copies ran while one was open for 3% -> 3% of each run, Pallas kernels for 0% -> 0%
where the time goes in v1:
time: 620 us; the launch traced here: 613 us
  waiting for transfers between devices  238 us (38%)
  matrix products  184 us (30%)
  local copies, waits for them, and re-layouts  78 us (13%)
  other arithmetic  68.7 us (11%)
  starting transfers between devices  22.8 us (4%)
  between operations  15.3 us (2%)
  loops' own time  6.43 us (1%)
    psum x1, waiting for transfers between devices, per_device(): lax.psum(lax.psum(block_here, axis_name='gy'), axis_name='gx')  119 us
    psum x1, waiting for transfers between devices, per_device(): lax.psum(block_here, axis_name='gy')  98.4 us
    scatter-add x2, other arithmetic, interact(): relative = src_pos[:, neighbour_ids] - own_pos[:, :, None]  34.7 us
    dot_general x6, matrix products, interact(): jnp.einsum('anc,xan->xac', weight_one * source, unit_vec, precision=highest)  27.5 us
    gather x4, local copies, waits for them, and re-layouts, interact(): source = h_src[neighbour_ids]  24.7 us
    dot_general x8, matrix products, structure_term(): imag_part = lax.dot_general(sine_part, charges, dims, precision=highest)  18.8 us
    dot_general x4, matrix products, interact(): jnp.einsum('anr,rc->anc', radial_basis, radial_pair[1], precision=highest)  18.8 us
    dot_general x8, matrix products, fold_terms(): jnp.dot(sine_part, weight_im, precision=highest)  18.7 us
  transfers between devices with their start and end apart: 18, of which 9 were waited for; matrix products, arithmetic and copies ran while one was open for 3% of the time, Pallas kernels for 0%

profile of v1, /device:TPU:127, one launch (start us, length us, event | category | flops | bytes accessed | tf_op | source)
XLA Modules:
  0.0 613.3 jit_solution(6820723377399730641)
XLA Ops:
  9.3 2.7 collective-permute-start
  17.3 4.3 collective-permute-start.2
  24.4 8.1 %gather_fusion = f32[3072,3]{1,0:T(8,128)S(1)} fusion(f32[3,2304]{0,1:T(8,128)S(1)} %bitcast.271, s32[3072]{0:T(1024)S(1)} %broadcast_clamp_fusion), kind=kCustom, calls=%fused_computation | custom fusion | bytes 86016 | tf_op jit(solution)/shard_map/jvp()/gather | solution.py:57
  36.6 10.8 %gather_fusion.1 = f32[3072,128]{1,0:T(8,128)} fusion(f32[2304,128]{1,0:T(8,128)S(1)} %fusion.133, s32[3072]{0:T(1024)S(1)} %broadcast_clamp_fusion), kind=kCustom, calls=%fused_computation.1 | custom fusion | bytes 3158016 | tf_op jit(solution)/shard_map/jvp()/gather | solution.py:72
  49.1 4.2 multiply_reduce_fusion.1
  53.3 4.4 multiply_multiply_fusion
  58.0 4.0 multiply_reduce_fusion.3
  62.3 2.9 collective-permute-start.4
  67.3 5.2 collective-permute-start.6
  72.5 5.0 convolution_multiply_fusion.1
  77.8 10.8 %gather_fusion.2 = f32[3072,128]{1,0:T(8,128)} fusion(f32[2304,128]{1,0:T(8,128)S(1)} %bitcast_convert_fusion, s32[3072]{0:T(1024)S(1)} %broadcast_clamp_fusion), kind=kCustom, calls=%fused_computation.2 | custom fusion | bytes 3158016 | tf_op jit(solution)/shard_map/jvp()/gather | solution.py:72
  90.1 6.9 %copy_multiply_fusion.1 = (f32[256,12,128]{2,0,1:T(8,128)S(1)}, f32[256,128]{1,0:T(8,128)S(1)}, f32[256,12,128]{2,0,1:T(8,128)}) fusion(f32[256,12,128]{2,1,0:T(8,128)S(1)} %reshape.168, f32[256,12,128]{2,0,1:T(8,128)} %convolution_multiply_fusion.1, f32[256,12]{0,1:T(8,128)S(1)} %fusion.161, f32[2,2,8,128]{3,2,1,0:T(8,128)} %param.21, ...), kind=kOutput, calls=%fused_computation.121 | convolution fusion | flops 39337984 | bytes 6451232 | tf_op jit(solution)/shard_map/jvp(anr,rc->anc)/dot_general | solution.py:69
  97.3 3.9 multiply_reduce_fusion.2
  102.4 62.0 %while.26 = (s32[]{:T(128)}, f32[8,512,128]{2,1,0:T(8,128)}, f32[3,256]{1,0:T(4,128)S(1)}, s32[8]{0:T(128)S(1)}, f32[3,4096]{1,0:T(4,128)}, /*index=5*/f32[256,6...) while((s32[]{:T(128)}, f32[8,512,128]{2,1,0:T(8,128)}, ...), condition=%wide.region_7.8_spmd, body=%wide.region_6.7_spmd.sunk | while | flops 202702848 | bytes 2003167 | solution.py:270
  164.5 98.4 %all-reduce.4.cloned.1.call-done = f32[4096,128]{1,0:T(8,128)} async-done(((f32[4096,128]{1,0:T(8,128)}), f32[4096,128]{1,0:T(8,128)}) %all-reduce.4.cloned.1.call-update) | async-done | bytes 2097168 | tf_op jit(solution)/shard_map/psum | solution.py:271
  264.1 119.0 %all-reduce.6.cloned.1.call-done = f32[4096,128]{1,0:T(8,128)} async-done(((f32[4096,128]{1,0:T(8,128)}), f32[4096,128]{1,0:T(8,128)}) %all-reduce.6.cloned.1.call-update) | async-done | bytes 2097168 | tf_op jit(solution)/shard_map/psum | solution.py:271
  385.3 87.4 %while.27 = (s32[]{:T(128)}, f32[256,64]{0,1:T(8,128)S(1)}, f32[3,256]{1,0:T(4,128)S(1)}, f32[3,256]{1,0:T(4,128)S(1)}, f32[3,4096]{1,0:T(4,128)}, /*index=5*/f3...) while((s32[]{:T(128)}, f32[256,64]{0,1:T(8,128)S(1)}, ...), condition=%wide.region_11.12_spmd.clone, body=%wide.region_10.11_spmd.clone.sunk | while | flops 410437120 | bytes 3739922 | solution.py:281
  474.8 4.0 fusion.88
  484.2 17.4 %scatter_fusion = f32[2304,128]{1,0:T(8,128)S(1)} fusion(f32[2304,128]{1,0:T(8,128)S(1)} %pad.3, s32[3072]{0:T(1024)S(1)} %reshape.153, f32[3072,128]{1,0:T(8,128)S(1)} %reshape.179), kind=kCustom, calls=%fused_computation.3 | custom fusion | flops 393216 | bytes 4730880 | tf_op jit(solution)/shard_map/transpose(jvp())/scatter-add | solution.py:72
  507.1 5.7 collective-permute-done.8
  512.8 3.3 collective-permute-done.9
  516.9 3.6 fusion.125
  523.2 4.1 fusion.47
  527.4 5.3 fusion.89
  532.7 6.2 %fusion.80 = (f32[256,12]{1,0:T(8,128)}, f32[256,12]{1,0:T(8,128)}, f32[256,3,12]{2,1,0:T(4,128)}) fusion(f32[256,12]{1,0:T(8,128)S(1)} %copy-done.30, f32[3,256]{0,1:T(8,128)S(1)} %copy.230, f32[256,12,3]{1,0,2:T(8,128)S(1)} %copy-done.13, f32[256,3,12]{2,1,0:T(4,128)S(1)} %fusion.47, f32[256,12,128]{2,0,1:T(8,128)S(1)} %copy-done.7, ...), kind=kOutput, calls=%fused_computation.110 | convolution fusion | flops 14509056 | bytes 2247680 | tf_op jit(solution)/shard_map/transpose(jvp(anc,xan->xac))/dot_general | solution.py:76
  542.1 3.9 fusion.52
  546.0 3.1 fusion.122
  549.5 3.0 fusion.201
  553.6 17.2 %scatter_custom_fusion.1 = f32[3,2304]{0,1:T(8,128)S(1)} fusion(s32[3072]{0:T(1024)S(1)} %reshape.153, f32[3072,3]{1,0:T(8,128)S(1)} %copy.264, f32[]{:T(128)} %constant.47.clone.1), kind=kCustom, calls=%fused_computation.107 | custom fusion | flops 9216 | bytes 27652 | tf_op jit(solution)/shard_map/transpose(jvp())/scatter-add | solution.py:57
  572.5 17.5 %scatter_custom_fusion.2 = f32[3,2304]{0,1:T(8,128)S(1)} fusion(s32[3072]{0:T(1024)S(1)} %reshape.153, f32[3072,3]{1,0:T(8,128)} %copy.266, f32[]{:T(128)} %constant.47.clone.1), kind=kCustom, calls=%fused_computation.105 | custom fusion | flops 9216 | bytes 28160 | tf_op jit(solution)/shard_map/transpose(jvp())/scatter-add | solution.py:57
  595.5 3.4 collective-permute-done.13
  602.2 3.5 collective-permute-done.15
  (343 shorter events, 199.6 us)
Async XLA Ops:
  7.2 256.6 %copy-start = (f32[128,128]{1,0:T(8,128)S(1)}, f32[128,128]{1,0:T(8,128)}, u32[]{:S(2)}) copy-start(f32[128,128]{1,0:T(8,128)} %param.23) | copy-start | bytes 196612
  7.2 255.8 %all-reduce.4.cloned.1.call-start = ((), (), s32[]{:S(2)}) async-start(), calls=%async_computation | async-start | bytes 4194304 | tf_op jit(solution)/shard_map/psum | solution.py:271
  8.6 7.5 %collective-permute-start.1 = (f32[1,1,4,256]{3,1,2,0:T(1,128)S(1)}, f32[1,1,4,256]{3,1,2,0:T(1,128)S(1)}, u32[]{:S(2)}, u32[]{:S(2)}) collective-permute-start(f32[1,1,4,256]{3,1,2,0:T(1,128)S(1)} %pad_maximum_fusion.5), channel_id=1, source_target_pairs={{16,0},{32,16},{48,32},{64,48},{80,64},{96,80},{112,96},{128,112},... | collective-permute-start | bytes 12296 | tf_op jit(solution)/shard_map/ppermute | solution.py:31
  9.3 6.8 %collective-permute-start = (f32[1,1,4,256]{3,1,2,0:T(1,128)S(1)}, f32[1,1,4,256]{3,1,2,0:T(1,128)S(1)}, u32[]{:S(2)}, u32[]{:S(2)}) collective-permute-start(f32[1,1,4,256]{3,1,2,0:T(1,128)S(1)} %pad_maximum_fusion.5), channel_id=1, source_target_pairs={{0,16},{16,32},{32,48},{48,64},{64,80},{80,96},{96,112},{112,128},... | collective-permute-start | bytes 12296 | tf_op jit(solution)/shard_map/ppermute | solution.py:28
  16.8 6.3 %collective-permute-start.3 = (f32[3,1,4,256]{3,1,2,0:T(1,128)S(1)}, f32[3,1,4,256]{3,1,2,0:T(1,128)S(1)}, u32[]{:S(2)}, u32[]{:S(2)}) collective-permute-start(f32[3,1,4,256]{3,1,2,0:T(1,128)S(1)} %pad_maximum_fusion.4), channel_id=1, source_target_pairs={{1,0},{2,1},{3,2},{4,3},{5,4},{6,5},{7,6},{8,7},{9,8},{10,9},{11,1... | collective-permute-start | bytes 36872 | tf_op jit(solution)/shard_map/ppermute | solution.py:31
  17.3 5.8 collective-permute-start.2
  49.0 8.6 %copy-start.4 = (f32[256,12,128]{2,1,0:T(8,128)}, f32[256,12,128]{2,1,0:T(8,128)S(1)}, u32[]{:S(2)}) copy-start(f32[256,12,128]{2,1,0:T(8,128)S(1)} %reshape.160) | copy-start | bytes 4718596
  58.0 7.3 %copy-start.39 = (f32[1,1,3,256]{3,1,2,0:T(1,128)S(1)}, f32[1,1,3,256]{3,1,2,0:T(1,128)}, u32[]{:S(2)}) copy-start(f32[1,1,3,256]{3,1,2,0:T(1,128)} %param.16) | copy-start | bytes 9220
  62.2 15.4 %copy-start.17 = (f32[256,128]{1,0:T(8,128)}, f32[256,128]{1,0:T(8,128)S(1)}, u32[]{:S(2)}) copy-start(f32[256,128]{1,0:T(8,128)S(1)} %convolution_add_fusion.5) | copy-start | bytes 393220
  62.3 4.9 collective-permute-start.5
  62.3 4.9 collective-permute-start.4
  67.2 10.3 %collective-permute-start.7 = (bf16[3,1,256,128]{3,2,1,0:T(8,128)(2,1)S(1)}, bf16[3,1,256,128]{3,2,1,0:T(8,128)(2,1)S(1)}, u32[]{:S(2)}, u32[]{:S(2)}) collective-permute-start(bf16[3,1,256,128]{3,2,1,0:T(8,128)(2,1)S(1)} %pad_maximum_fusion.1), channel_id=1, source_target_pairs={{1,0},{2,1},{3,2},{4,3},{5,4},{6,5},{7,6},{8,7},{9,8},{10,9},{11,1... | collective-permute-start | bytes 589832 | tf_op jit(solution)/shard_map/ppermute | solution.py:31
  67.3 10.2 %collective-permute-start.6 = (bf16[3,1,256,128]{3,2,1,0:T(8,128)(2,1)S(1)}, bf16[3,1,256,128]{3,2,1,0:T(8,128)(2,1)S(1)}, u32[]{:S(2)}, u32[]{:S(2)}) collective-permute-start(bf16[3,1,256,128]{3,2,1,0:T(8,128)(2,1)S(1)} %pad_maximum_fusion.1), channel_id=1, source_target_pairs={{0,1},{1,2},{2,3},{3,4},{4,5},{5,6},{6,7},{7,8},{8,9},{9,10},{10,1... | collective-permute-start | bytes 589832 | tf_op jit(solution)/shard_map/ppermute | solution.py:28
  164.4 98.6 %copy-start.44 = (f32[4096]{0:T(1024)S(1)}, f32[4096]{0:T(1024)}, u32[]{:S(2)}) copy-start(f32[4096]{0:T(1024)} %get-tuple-element.319) | copy-start | bytes 49156
  164.4 98.6 %copy-start.41 = (f32[256,12]{0,1:T(8,128)S(1)}, f32[256,12]{0,1:T(8,128)}, u32[]{:S(2)}) copy-start(f32[256,12]{0,1:T(8,128)} %get-tuple-element.345) | copy-start | bytes 36868
  164.4 218.6 %all-reduce.6.cloned.1.call-start = ((), (), s32[]{:S(2)}) async-start(), calls=%async_computation.1 | async-start | bytes 4194304 | tf_op jit(solution)/shard_map/psum | solution.py:271
  264.1 209.0 %copy-start.52 = (f32[256,128]{1,0:T(8,128)}, f32[256,128]{1,0:T(8,128)S(1)}, u32[]{:S(2)}) copy-start(f32[256,128]{1,0:T(8,128)S(1)} %fusion.196) | copy-start | bytes 393220
  385.3 88.0 %copy-start.50 = (f32[128]{0:T(128)S(1)}, f32[128]{0:T(128)}, u32[]{:S(2)}) copy-start(f32[128]{0:T(128)} %param.24) | copy-start | bytes 1540
  385.3 88.3 %copy-start.21 = (f32[2,2,128,128]{3,2,1,0:T(8,128)S(1)}, f32[2,2,128,128]{3,2,1,0:T(8,128)}, u32[]{:S(2)}) copy-start(f32[2,2,128,128]{3,2,1,0:T(8,128)} %param.22) | copy-start | bytes 786436
  484.1 19.0 %copy-start.51 = (f32[128]{0:T(128)S(1)}, f32[128]{0:T(128)}, u32[]{:S(2)}) copy-start(f32[128]{0:T(128)} %param.24) | copy-start | bytes 1540
  501.6 11.2 %collective-permute-start.8 = (f32[3,256,128]{2,1,0:T(8,128)S(1)}, f32[3,256,128]{2,1,0:T(8,128)S(1)}, u32[]{:S(2)}, u32[]{:S(2)}) collective-permute-start(f32[3,256,128]{2,1,0:T(8,128)S(1)} %get-tuple-element.335), channel_id=1, source_target_pairs={{15,0},{0,1},{1,2},{2,3},{3,4},{4,5},{5,6},{6,7},{7,8},{8,9},{9,10... | collective-permute-start | bytes 1179656 | tf_op jit(solution)/shard_map/ppermute | solution.py:19
  501.9 14.2 %collective-permute-start.9 = (f32[3,256,128]{2,1,0:T(8,128)S(1)}, f32[3,256,128]{2,1,0:T(8,128)S(1)}, u32[]{:S(2)}, u32[]{:S(2)}) collective-permute-start(f32[3,256,128]{2,1,0:T(8,128)S(1)} %get-tuple-element.336), channel_id=1, source_target_pairs={{1,0},{2,1},{3,2},{4,3},{5,4},{6,5},{7,6},{8,7},{9,8},{10,9},{11,1... | collective-permute-start | bytes 1179656 | tf_op jit(solution)/shard_map/ppermute | solution.py:19
  504.9 12.0 %copy-start.15 = (f32[256,12,128]{2,1,0:T(8,128)S(1)}, f32[256,12,128]{2,1,0:T(8,128)}, u32[]{:S(2)}) copy-start(f32[256,12,128]{2,1,0:T(8,128)} %copy-done.14) | copy-start | bytes 4718596
  516.2 4.4 collective-permute-start.10
  516.3 5.6 collective-permute-start.11
  532.6 9.4 %copy-start.5 = (f32[256,12,128]{2,1,0:T(8,128)S(1)}, f32[256,12,128]{2,1,0:T(8,128)}, u32[]{:S(2)}) copy-start(f32[256,12,128]{2,1,0:T(8,128)} %copy-done.4) | copy-start | bytes 4718596
  590.1 11.4 %copy-start.49 = (f32[1,256]{1,0:T(1,128)S(1)}, f32[1,256]{1,0:T(1,128)}, u32[]{:S(2)}) copy-start(f32[1,256]{1,0:T(1,128)} %fusion.112) | copy-start | bytes 3076
  590.1 11.9 %copy-start.31 = (f32[3,256]{0,1:T(8,128)S(1)}, f32[3,256]{0,1:T(8,128)}, u32[]{:S(2)}) copy-start(f32[3,256]{0,1:T(8,128)} %get-tuple-element.317) | copy-start | bytes 9220
  592.9 2.6 collective-permute-start.12
  593.1 5.9 collective-permute-start.13
  599.0 3.2 collective-permute-start.14
  601.4 4.2 collective-permute-start.15
  (39 other events, 164.3 us)
Sparse Core Ops, SparseCore 0:
  164.5 98.3 all-reduce.3
  265.4 117.6 all-reduce.5
